TPU v7x, 32 devices: a whole 2x2x4 slice. The times are simulated.
32 devices in a mesh: sx: 8 (over y, x, core), sy: 4 (over z).
Axes of the slice: x: 2, y: 2, z: 4, core: 2. Of those that a mesh axis runs over, the one named last changes fastest.
Arguments:
- tokens: bfloat16 [16384, 1024], P(('sx', 'sy')), may hold values from -6 to 6
- norm_gain: float32 [1024], replicated, may hold values from 0.1 to 1.9
- w_qk: bfloat16 [1024, 1024], replicated, may hold values from -1.75 to 1.75
- w_value: bfloat16 [1024, 1024], replicated, may hold values from -0.1875 to 0.1875
- w_out: bfloat16 [1024, 1024], replicated, may hold values from -0.1875 to 0.1875
- send_order: int32 [8, 16384], P(None, ('sx', 'sy')), may hold values from 0 to 511, as said below
- place: int32 [8, 16384], P(None, ('sx', 'sy')), may hold values from 0 to 511, as said below
Outputs:
- attended: bfloat16 [16384, 1024], P(('sx', 'sy'))
Inputs may be any that keep to these rules, and one draw needn't show every extreme that they name: `send_order`: for every head and every device, the device's 512 entries form a permutation of 0 to 511. `place`: for every head and every device, the device's 512 entries form a permutation of 0 to 511.
All inputs are finite; a program needn't handle non-finite values.
Results may differ from a plain program's by a relative error of at most 0.012.
The roundings to bfloat16 on the way count: a program that leaves them out, or rounds other values in their place, can miss the bound.
Values may be sent and summed in bfloat16 or wider, within the bound.
No kernel may reach another device: no remote copies, remote signals or barrier semaphores. Data moves between devices by JAX's collectives and lax.ppermute only.
A program may use at most 64 MiB of HBM per device.

v0:
```python
import jax
import jax.numpy as jnp
from jax import lax
from jax.sharding import PartitionSpec as P

HEADS = 8
HEAD_DIM = 128
SPAN = 128


def shifted(array, axis, by):
    peers = lax.axis_size(axis)
    return lax.ppermute(array, axis, [(i, (i + by) % peers) for i in range(peers)])


def route_out(buffer):
    return lax.all_to_all(buffer, ("sx", "sy"), split_axis=1, concat_axis=1, tiled=True)


def route_back(buffer):
    return lax.all_to_all(buffer, ("sx", "sy"), split_axis=1, concat_axis=1, tiled=True)


def attend_spans(current, previous):
    window = jnp.concatenate([previous, current], axis=2)
    query = current[..., :HEAD_DIM]
    keys = window[..., :HEAD_DIM].astype(jnp.float32)
    key_stat = jnp.sum(keys * keys, -1, keepdims=True) + 1e-06
    unit = (keys * lax.rsqrt(key_stat)).astype(jnp.bfloat16)
    scores = jnp.einsum(
        "hcqd,hckd->hcqk", query, unit, preferred_element_type=jnp.float32
    ) * HEAD_DIM ** (-0.5)
    rows = jnp.arange(SPAN)[:, None]
    cols = jnp.arange(2 * SPAN)[None, :]
    scores = jnp.where(cols == rows + SPAN, -100000.0, scores)
    weights = jax.nn.softmax(scores, axis=-1).astype(jnp.bfloat16)
    return jnp.einsum(
        "hcqk,hckd->hcqd", weights, window[..., HEAD_DIM:], preferred_element_type=jnp.float32
    ).astype(jnp.bfloat16)


def per_device(tokens, norm_gain, w_qk, w_value, w_out, send_order, place):
    tok_rows = tokens.shape[0]
    devices = lax.axis_size(("sx", "sy"))
    peer = tok_rows // devices
    floats = tokens.astype(jnp.float32)
    row_stat = jnp.mean(floats * floats, -1, keepdims=True) + 1e-06
    scale = lax.rsqrt(row_stat)
    normed = (floats * scale * norm_gain).astype(jnp.bfloat16)
    shared = jnp.dot(normed, w_qk, preferred_element_type=jnp.float32).astype(jnp.bfloat16)
    values = jnp.dot(normed, w_value, preferred_element_type=jnp.float32).astype(jnp.bfloat16)
    stacked = jnp.concatenate(
        [shared.reshape(tok_rows, HEADS, HEAD_DIM), values.reshape(tok_rows, HEADS, HEAD_DIM)], -1
    )
    columns = jnp.arange(tok_rows, dtype=jnp.int32)[None, None, :]
    send_table = (send_order[:, :, None] == columns).astype(jnp.bfloat16)
    place_table = (place[:, :, None] == columns).astype(jnp.bfloat16)
    outgoing = jnp.einsum(
        "hit,thc->hic", send_table, stacked, preferred_element_type=jnp.float32
    ).astype(jnp.bfloat16)
    arrived = route_out(outgoing.reshape(HEADS, devices, peer, 2 * HEAD_DIM)).reshape(
        HEADS, tok_rows, 2 * HEAD_DIM
    )
    ordered = jnp.einsum(
        "hip,hic->hpc", place_table, arrived, preferred_element_type=jnp.float32
    ).astype(jnp.bfloat16)
    last_span = ordered[:, tok_rows - SPAN :]
    edge = shifted(last_span, ("sx", "sy"), 1)
    spans = ordered.reshape(HEADS, tok_rows // SPAN, SPAN, 2 * HEAD_DIM)
    previous = jnp.concatenate([edge[:, None], spans[:, :-1]], axis=1)
    sorted_out = attend_spans(spans, previous).reshape(HEADS, tok_rows, HEAD_DIM)
    leaving = jnp.einsum(
        "hip,hpc->hic", place_table, sorted_out, preferred_element_type=jnp.float32
    ).astype(jnp.bfloat16)
    returned = route_back(leaving.reshape(HEADS, devices, peer, HEAD_DIM)).reshape(
        HEADS, tok_rows, HEAD_DIM
    )
    merged = jnp.einsum(
        "hit,hic->thc", send_table, returned, preferred_element_type=jnp.float32
    ).astype(jnp.bfloat16)
    merged = merged.reshape(tok_rows, HEADS * HEAD_DIM)
    return jnp.dot(merged, w_out, preferred_element_type=jnp.float32).astype(jnp.bfloat16)


def solution(mesh):
    return jax.shard_map(
        per_device,
        mesh=mesh,
        in_specs=(
            P(("sx", "sy"), None),
            P(),
            P(),
            P(),
            P(),
            P(None, ("sx", "sy")),
            P(None, ("sx", "sy")),
        ),
        out_specs=P(("sx", "sy"), None),
        check_vma=False,
    )
```

profile of v0, /device:TPU:1, one launch (start us, length us, event | category | flops | bytes accessed | tf_op | source)
XLA Modules:
  0.0 127.2 jit_solution(5826174542858874339)
XLA Ops:
  0.0 1.7 %fusion.12 = f32[512]{0:T(512)S(1)} fusion(bf16[512,1024]{1,0:T(8,128)(2,1)} %param.7), kind=kLoop, calls=%fused_computation.22 | loop fusion | flops 1572352 | bytes 1050624 | tf_op jit(solution)/shard_map/reduce_sum | solution.py:47
  1.7 0.2 copy-done
  1.9 2.7 %fusion.37 = bf16[64,8,8,128]{3,2,1,0:T(8,128)(2,1)S(1)} fusion(bf16[1024,1024]{1,0:T(8,128)(2,1)S(1)} %copy-done, bf16[512,1024]{1,0:T(8,128)(2,1)} %param.7, f32[1024]{0:T(1024)} %param.8, f32[512]{0:T(512)S(1)} %add_rsqrt_fusion.1), kind=kOutput, calls=%fused_computation.45 | convolution fusion | flops 1076363264 | bytes 4200448 | tf_op jit(solution)/shard_map/dot_general | solution.py:51
  4.6 1.3 %fusion.36 = bf16[64,8,8,128]{3,2,1,0:T(8,128)(2,1)S(1)} fusion(bf16[1024,1024]{1,0:T(8,128)(2,1)S(1)} %copy-done.3, bf16[512,1024]{1,0:T(8,128)(2,1)S(1)} %copy-done.2, f32[1024]{0:T(1024)S(1)} %copy-done.6, f32[512]{0:T(512)S(1)} %add_rsqrt_fusion.1), kind=kOutput, calls=%fused_computation.44 | convolution fusion | flops 1076363264 | bytes 4200448 | tf_op jit(solution)/shard_map/dot_general | solution.py:50
  6.0 0.5 copy_bitcast_fusion
  6.4 0.2 copy-done.5
  6.7 2.1 %fusion.27 = bf16[8,512,256]{2,1,0:T(8,128)(2,1)S(1)} fusion(bf16[512,8,128]{2,0,1:T(8,128)(2,1)S(1)} %get-tuple-element.7, bf16[512,8,128]{2,0,1:T(8,128)(2,1)S(1)} %get-tuple-element.8, s32[8,512]{1,0:T(8,128)S(1)} %copy-done.5), kind=kOutput, calls=%fused_computation.36 | convolution fusion | flops 1081081856 | bytes 4210688 | tf_op jit(solution)/shard_map/hit,thc->hic/dot_general | solution.py:58
  8.8 0.3 copy.20
  9.1 55.7 %all_to_all.10 = bf16[8,32,16,256]{3,2,0,1:T(8,128)(2,1)S(1)} all-to-all(bf16[8,32,16,256]{3,2,0,1:T(8,128)(2,1)S(1)} %copy.20), channel_id=1, replica_groups=mesh['sx'=8,'sy'=4] {'sx','sy'}, dimensions={1} | all-to-all | bytes 4194304 | tf_op jit(solution)/shard_map/all_to_all | solution.py:17
  64.8 0.2 copy.21
  65.0 0.5 copy-done.4
  65.5 3.2 %fusion.26 = bf16[8,512,256]{2,1,0:T(8,128)(2,1)S(1)} fusion(bf16[8,512,256]{2,1,0:T(8,128)(2,1)S(1)} %bitcast.31, s32[8,512]{1,0:T(8,128)S(1)} %copy-done.4), kind=kOutput, calls=%fused_computation.35 | convolution fusion | flops 1076887552 | bytes 4210688 | tf_op jit(solution)/shard_map/hip,hic->hpc/dot_general | solution.py:64
  69.1 15.2 %collective-permute-done = bf16[8,128,256]{2,1,0:T(8,128)(2,1)S(1)} collective-permute-done((bf16[8,128,256]{2,1,0:T(8,128)(2,1)S(1)}, bf16[8,128,256]{2,1,0:T(8,128)(2,1)S(1)}, u32[]{:S(2)}, u32[]{:S(2)}) %collective-permute-start) | collective-permute-done | bytes 524320 | tf_op jit(solution)/shard_map/ppermute | solution.py:13
  84.3 0.5 pad_maximum_fusion
  84.8 1.2 fusion.5
  86.0 3.1 %fusion.15 = f32[8,4,128,256]{3,2,1,0:T(8,128)S(1)} fusion(f32[8,4,256]{2,1,0:T(4,128)S(1)} %add_rsqrt_fusion, bf16[8,4,256,256]{3,2,1,0:T(8,128)(2,1)S(1)} %pad_maximum_fusion, bf16[8,4,128,256]{3,2,1,0:T(8,128)(2,1)S(1)} %bitcast.29), kind=kOutput, calls=%fused_computation.25 | convolution fusion | flops 271581184 | bytes 7372800 | tf_op jit(solution)/shard_map/hcqd,hckd->hcqk/dot_general | solution.py:30
  89.1 2.0 %fusion.44 = (f32[8,4,128]{2,1,0:T(4,128)S(1)}, f32[8,4,128,256]{3,2,1,0:T(8,128)S(1)}) fusion(f32[8,4,128,256]{3,2,1,0:T(8,128)S(1)} %fusion.15, pred[128,256]{1,0:T(8,128)(4,1)S(1)} %iota_compare_fusion.14), kind=kOutput, calls=%fused_computation.56 | output fusion | flops 6291711 | bytes 8437760 | tf_op jit(solution)/shard_map/sub | solution.py:36
  91.1 1.0 fusion.33
  92.1 1.8 %fusion.31 = bf16[8,512,128]{2,1,0:T(8,128)(2,1)S(1)} fusion(bf16[8,512,128]{2,1,0:T(8,128)(2,1)S(1)} %bitcast.36, s32[8,512]{1,0:T(8,128)S(1)} %copy-done.4), kind=kOutput, calls=%fused_computation.38 | convolution fusion | flops 539492352 | bytes 2113536 | tf_op jit(solution)/shard_map/hip,hpc->hic/dot_general | solution.py:72
  93.9 0.3 copy.24
  94.2 28.3 %all_to_all.11 = bf16[8,32,16,128]{3,2,0,1:T(8,128)(2,1)S(1)} all-to-all(bf16[8,32,16,128]{3,2,0,1:T(8,128)(2,1)S(1)} %copy.24), channel_id=1, replica_groups=mesh['sx'=8,'sy'=4] {'sx','sy'}, dimensions={1} | all-to-all | bytes 2097152 | tf_op jit(solution)/shard_map/all_to_all | solution.py:21
  122.5 0.2 copy.25
  122.7 2.2 %fusion.32 = bf16[8,128,512]{2,1,0:T(8,128)(2,1)S(1)} fusion(bf16[8,512,128]{2,1,0:T(8,128)(2,1)S(1)} %bitcast.33, s32[8,512]{1,0:T(8,128)S(1)} %copy-done.5), kind=kOutput, calls=%fused_computation.39 | convolution fusion | flops 539492352 | bytes 2113536 | tf_op jit(solution)/shard_map/hit,hic->thc/dot_general | solution.py:78
  124.9 2.2 %convolution_convert_fusion = bf16[512,1024]{1,0:T(8,128)(2,1)} fusion(bf16[512,1024]{0,1:T(8,128)(2,1)S(1)} %bitcast.34, bf16[1024,1024]{1,0:T(8,128)(2,1)S(1)} %copy-done.1), kind=kOutput, calls=%fused_computation.40 | convolution fusion | flops 1074266112 | bytes 4194304 | tf_op jit(solution)/shard_map/dot_general | solution.py:82
  (18 shorter events, 0.4 us)
Async XLA Ops:
  0.0 1.9 %copy-start = (bf16[1024,1024]{1,0:T(8,128)(2,1)S(1)}, bf16[1024,1024]{1,0:T(8,128)(2,1)}, u32[]{:S(2)}) copy-start(bf16[1024,1024]{1,0:T(8,128)(2,1)} %param.10) | copy-start | bytes 6291460
  1.9 2.7 %copy-start.2 = (bf16[512,1024]{1,0:T(8,128)(2,1)S(1)}, bf16[512,1024]{1,0:T(8,128)(2,1)}, u32[]{:S(2)}) copy-start(bf16[512,1024]{1,0:T(8,128)(2,1)} %param.7) | copy-start | bytes 3145732
  1.9 2.7 %copy-start.3 = (bf16[1024,1024]{1,0:T(8,128)(2,1)S(1)}, bf16[1024,1024]{1,0:T(8,128)(2,1)}, u32[]{:S(2)}) copy-start(bf16[1024,1024]{1,0:T(8,128)(2,1)} %param.9) | copy-start | bytes 6291460
  1.9 2.7 %copy-start.6 = (f32[1024]{0:T(1024)S(1)}, f32[1024]{0:T(1024)}, u32[]{:S(2)}) copy-start(f32[1024]{0:T(1024)} %param.8) | copy-start | bytes 12292
  5.9 0.7 copy-start.5
  64.8 0.7 copy-start.4
  68.7 15.5 %collective-permute-start = (bf16[8,128,256]{2,1,0:T(8,128)(2,1)S(1)}, bf16[8,128,256]{2,1,0:T(8,128)(2,1)S(1)}, u32[]{:S(2)}, u32[]{:S(2)}) collective-permute-start(bf16[8,128,256]{2,1,0:T(8,128)(2,1)S(1)} %slice.21), channel_id=1, source_target_pairs={{0,1},{1,2},{2,3},{3,4},{4,5},{5,6},{6,7},{7,8},{8,9},{9,10},{10,1... | collective-permute-start | bytes 1572872 | tf_op jit(solution)/shard_map/ppermute | solution.py:13
  122.7 2.2 %copy-start.1 = (bf16[1024,1024]{1,0:T(8,128)(2,1)S(1)}, bf16[1024,1024]{1,0:T(8,128)(2,1)}, u32[]{:S(2)}) copy-start(bf16[1024,1024]{1,0:T(8,128)(2,1)} %param.11) | copy-start | bytes 6291460
where the time goes:
time: 128 us; the launch traced here: 127 us
  blocking collectives  84 us (66%)
  matrix products  19.6 us (15%)
  waiting for transfers between devices  15.2 us (12%)
  other arithmetic  5.44 us (4%)
  local copies, waits for them, and re-layouts  2.6 us (2%)
    all_to_all x1, blocking collectives, route_out(): lax.all_to_all(buffer, ('sx', 'sy'), split_axis=1, concat_axis=1, tiled=T...  55.7 us
    all_to_all x1, blocking collectives, route_back(): lax.all_to_all(buffer, ('sx', 'sy'), split_axis=1, concat_axis=1, tiled=T...  28.3 us
    ppermute x1, waiting for transfers between devices, shifted(): lax.ppermute(array, axis, [(i, (i + by) % peers) for i in range(peers)])  15.2 us
    dot_general x1, matrix products, per_device(): jnp.einsum('hip,hic->hpc', place_table, arrived, preferred_element_type=j...  3.15 us
    dot_general x1, matrix products, attend_spans(): jnp.einsum('hcqd,hckd->hcqk', query, unit, preferred_element_type=jnp.flo...  3.12 us
    dot_general x1, matrix products, per_device(): jnp.dot(normed, w_value, preferred_element_type=jnp.float32)  2.68 us
  transfers between devices with their start and end apart: 1, of which 1 were waited for; matrix products, arithmetic and copies ran while one was open for 0% of the time, Pallas kernels for 0%

commit v1 on v0

v1 whole, which is shorter than its diff:
```python
import functools

import jax
import jax.numpy as jnp
from jax import lax
from jax.experimental import pallas as pl
from jax.experimental.pallas import tpu as pltpu
from jax.sharding import PartitionSpec as P

HEADS = 8
HEAD_DIM = 128
SPAN = 128
WIDTH = 2 * HEAD_DIM
AXES = ("sx", "sy")
BLOCKS_ALONG = ("sy", "sx")
MIB = 1024 * 1024
LONG = 10**12
BF16 = jnp.bfloat16
F32 = jnp.float32
ANY = pl.BlockSpec(memory_space=pl.ANY)
HBM = pl.BlockSpec(memory_space=pltpu.HBM)
VMEM = pl.BlockSpec(memory_space=pltpu.VMEM)


def dot(a, b):
    return jnp.dot(a, b, preferred_element_type=F32)


def by_column(column, size):
    lanes = lax.broadcasted_iota(jnp.int32, (column.shape[0], size), 1)
    return jnp.where(lanes == column, 1.0, 0.0).astype(BF16)


def by_row(row, first, size):
    sublanes = lax.broadcasted_iota(jnp.int32, (size, row.shape[1]), 0) + first
    return jnp.where(sublanes == row, 1.0, 0.0).astype(BF16)


def rolled(table, by):
    return pltpu.roll(table, by % table.shape[1], 1)


def relative(table, peer):
    lanes = lax.broadcasted_iota(jnp.int32, table.shape, 1)
    me = (lax.axis_index("sy") * lax.axis_size("sx") + lax.axis_index("sx")) * peer
    bit = peer
    while bit < table.shape[1]:
        other = jnp.where((lanes & bit) == 0, rolled(table, -bit), rolled(table, bit))
        table = jnp.where((me & bit) > 0, other, table)
        bit *= 2
    return table


def axes_swapped(table, minor, peer):
    lanes = lax.broadcasted_iota(jnp.int32, table.shape, 1)
    minor_bits = lax.axis_size(minor).bit_length() - 1
    major_bits = (table.shape[1] // peer).bit_length() - 1 - minor_bits
    now = list(range(major_bits + minor_bits))
    goal = [major_bits + j for j in range(minor_bits)] + list(range(major_bits))
    for j in range(len(goal)):
        if now[j] == goal[j]:
            continue
        low, high = sorted((now[j], goal[j]))
        low_bit, high_bit = peer << low, peer << high
        has_low, has_high = (lanes & low_bit) > 0, (lanes & high_bit) > 0
        down = rolled(table, low_bit - high_bit)
        up = rolled(table, high_bit - low_bit)
        table = jnp.where(has_low == has_high, table, jnp.where(has_low, down, up))
        now = [{low: high, high: low}.get(v, v) for v in now]
    return table


def to_columns(table):
    filler = jnp.zeros((128 - table.shape[0], table.shape[1]), table.dtype)
    return jnp.concatenate([table, filler], 0).T


def call(body, outs, scratch=(), specs=None, out_specs=None, cost=0, limit=40, after=()):
    count = [0]

    def skipping(*refs):
        return body(*refs[: count[0]], *refs[count[0] + len(after) :])

    def wrapped(*args):
        count[0] = len(args)
        return pl.pallas_call(
            skipping,
            out_shape=[jax.ShapeDtypeStruct(s, d) for s, d in outs],
            in_specs=([VMEM] * len(args) if specs is None else specs) + [ANY] * len(after),
            out_specs=[VMEM] * len(outs) if out_specs is None else out_specs,
            scratch_shapes=list(scratch),
            compiler_params=pltpu.CompilerParams(vmem_limit_bytes=limit * MIB),
            cost_estimate=pl.CostEstimate(flops=cost, bytes_accessed=0, transcendentals=0),
        )(*args, *after)

    return wrapped


BLOCKS = 4


def project_body(first, heads, order, peer, tokens, gain, send, w_qk, w_value, *rest):
    outs, (held, weights, token_sems, sems) = rest[:-4], rest[-4:]
    rows = held.shape[0]
    block = rows // BLOCKS
    loads = []
    for i in range(BLOCKS):
        part = pl.ds(i * block, block)
        loads.append(pltpu.make_async_copy(tokens.at[part], held.at[part], token_sems.at[i]))
        loads[-1].start()
    copies = []
    for h in range(heads):
        cols = pl.ds((first + h) * HEAD_DIM, HEAD_DIM)
        for j, source in enumerate((w_qk, w_value)):
            copy = pltpu.make_async_copy(
                source.at[:, cols],
                weights.at[h, :, pl.ds(j * HEAD_DIM, HEAD_DIM)],
                sems.at[2 * h + j],
            )
            copy.start()
            copies.append(copy)
    columns = to_columns(ordered_table(send[...], order, peer))
    normed = []
    for i in range(BLOCKS):
        loads[i].wait()
        floats = held[i * block : (i + 1) * block].astype(F32)
        stat = jnp.sum(floats * floats, -1, keepdims=True) * (1.0 / floats.shape[1]) + 1e-06
        normed.append((floats * lax.rsqrt(stat) * gain[...]).astype(BF16))
    normed = jnp.concatenate(normed, 0)
    for h in range(heads):
        copies[2 * h].wait()
        copies[2 * h + 1].wait()
        both = dot(normed, weights[h]).astype(BF16)
        moved = dot(by_column(columns[:, first + h : first + h + 1], rows), both).astype(BF16)
        store_rows(outs, moved, h, order, peer)


def store_rows(outs, moved, h, order, peer):
    rows = moved.shape[0]
    if order:
        part = rows // len(outs)
        for r, out in enumerate(outs):
            out[h] = moved[r * part : (r + 1) * part]
    elif peer % 16:
        outs[0][h] = moved
    else:
        for d in range(rows // peer):
            outs[0][d, h * peer : (h + 1) * peer] = moved[d * peer : (d + 1) * peer]


def row_outs(rows, heads, width, order, peer):
    if order:
        pieces = lax.axis_size("s" + order)
        return [((heads, rows // pieces, width), BF16)] * pieces
    if peer % 16:
        return [((heads, rows, width), BF16)]
    return [((rows // peer, heads * peer, width), BF16)]


def project(tokens, gain, send, w_qk, w_value, first, heads, order, peer, after=()):
    rows, depth = tokens.shape
    return call(
        functools.partial(project_body, first, heads, order, peer),
        row_outs(rows, heads, WIDTH, order, peer),
        scratch=[
            pltpu.VMEM((rows, depth), BF16),
            pltpu.VMEM((heads, depth, WIDTH), BF16),
            pltpu.SemaphoreType.DMA((BLOCKS,)),
            pltpu.SemaphoreType.DMA((2 * heads,)),
        ],
        specs=[HBM, VMEM, VMEM, HBM, HBM],
        limit=63,
        after=after,
    )(tokens, gain.reshape(1, depth), send, w_qk, w_value)


def arrived_rows(pieces, h, heads):
    if len(pieces) == 1 and pieces[0].shape[0] != heads:
        peer = pieces[0].shape[1] // heads
        own = slice(h * peer, (h + 1) * peer)
        return jnp.concatenate([pieces[0][d, own] for d in range(pieces[0].shape[0])], 0)
    return jnp.concatenate([p[h] for p in pieces], 0)


def ordered_table(table, order, peer):
    if order:
        table = relative(table, peer)
    return axes_swapped(table, "sx", peer) if order == "x" else table


def edge_body(first, order, peer, *refs):
    place, pieces, out = refs[0], refs[1:-1], refs[-1]
    rows = place.shape[1]
    index = ordered_table(axes_swapped(place[...], "sy", peer), order, peer)
    for h in range(out.shape[0]):
        table = by_row(index[first + h : first + h + 1, :], rows - SPAN, SPAN)
        out[h] = dot(table, arrived_rows(pieces, h, out.shape[0])).astype(BF16)


def unit_keys(shared):
    keys = shared.astype(F32)
    stat = jnp.sum(keys * keys, -1, keepdims=True) + 1e-06
    return (keys * lax.rsqrt(stat)).astype(BF16)


def one_span(query, unit, values):
    scores = lax.dot_general(query, unit, (((1,), (1,)), ((), ())), preferred_element_type=F32)
    scores = scores * HEAD_DIM ** (-0.5)
    rows = lax.broadcasted_iota(jnp.int32, scores.shape, 0)
    cols = lax.broadcasted_iota(jnp.int32, scores.shape, 1)
    scores = jnp.where(cols == rows + SPAN, -100000.0, scores)
    powers = jnp.exp(scores - jnp.max(scores, -1, keepdims=True))
    weights = (powers * (1.0 / jnp.sum(powers, -1, keepdims=True))).astype(BF16)
    return dot(weights, values).astype(BF16)


def inner_body(first, order, peer, *refs):
    place, edge, pieces, (head_span, out) = refs[0], refs[1], refs[2:-2], refs[-2:]
    rows = place.shape[1]
    index = ordered_table(axes_swapped(place[...], "sy", peer), order, peer)
    for h in range(out.shape[0]):
        table = by_row(index[first + h : first + h + 1, :], 0, rows - SPAN)
        ordered = dot(table, arrived_rows(pieces, h, out.shape[0])).astype(BF16)
        head_span[h] = ordered[:SPAN]
        ordered = jnp.concatenate([ordered, edge[h]], 0)
        unit = unit_keys(ordered[:, :HEAD_DIM])
        for c in range(1, rows // SPAN):
            window = slice((c - 1) * SPAN, (c + 1) * SPAN)
            out[h, (c - 1) * SPAN : c * SPAN] = one_span(
                ordered[c * SPAN : (c + 1) * SPAN, :HEAD_DIM], unit[window], ordered[window, HEAD_DIM:]
            )


def outer_body(first, order, peer, *refs):
    place, before, head_span, inner, outs = refs[0], refs[1], refs[2], refs[3], refs[4:]
    rows = place.shape[1]
    table = axes_swapped(place[...], "sy", peer)
    columns = to_columns(ordered_table(table, order, peer))
    for h in range(inner.shape[0]):
        window = jnp.concatenate([before[h], head_span[h]], 0)
        unit = unit_keys(window[:, :HEAD_DIM])
        attended = one_span(head_span[h, :, :HEAD_DIM], unit, window[:, HEAD_DIM:])
        attended = jnp.concatenate([attended, inner[h]], 0)
        moved = dot(by_column(columns[:, first + h : first + h + 1], rows), attended).astype(BF16)
        store_rows(outs, moved, h, order, peer)


def worker(block):
    n_sx, n_sy = lax.axis_size("sx"), lax.axis_size("sy")
    return block % n_sx * n_sy + block // n_sx


def attention(place, arrived, arrived_order, first, heads, order, peer, cost, after=()):
    rows = place.shape[1]
    (edge,) = call(
        functools.partial(edge_body, first, arrived_order, peer),
        [((heads, SPAN, WIDTH), BF16)],
        cost=cost,
        after=after,
    )(place, *arrived)
    peers = lax.axis_size(AXES)
    before = lax.ppermute(edge, AXES, [(worker(d), worker((d + 1) % peers)) for d in range(peers)])
    head_span, inner = call(
        functools.partial(inner_body, first, arrived_order, peer),
        [((heads, SPAN, WIDTH), BF16), ((heads, rows - SPAN, HEAD_DIM), BF16)],
        cost=cost,
    )(place, edge, *arrived)
    return call(
        functools.partial(outer_body, first, order, peer),
        row_outs(rows, heads, HEAD_DIM, order, peer),
        cost=cost,
    )(place, before, head_span, inner)


def merge_body(first, heads, order, peer, n_pieces, send, w_out, *rest):
    pieces, total, (out, weights, weight_sem) = rest[:n_pieces], rest[n_pieces:-3], rest[-3:]
    width = heads * HEAD_DIM
    load = pltpu.make_async_copy(w_out.at[pl.ds(first * HEAD_DIM, width)], weights, weight_sem)
    load.start()
    rows = send.shape[1]
    index = ordered_table(send[...], order, peer)
    merged = []
    for h in range(heads):
        table = by_row(index[first + h : first + h + 1, :], 0, rows)
        merged.append(dot(table, arrived_rows(pieces, h, heads)).astype(BF16))
    merged = jnp.concatenate(merged, 1)
    load.wait()
    result = dot(merged, weights[...])
    if total:
        result = result + total[0][...]
    out[...] = result.astype(out.dtype)


def merge(send, w_out, total, pieces, first, heads, order, peer, cost, after=()):
    rows, depth = send.shape[1], w_out.shape[1]
    width = heads * HEAD_DIM
    extra = [] if total is None else [total]
    (out,) = call(
        functools.partial(merge_body, first, heads, order, peer, len(pieces)),
        [((rows, depth), BF16)],
        scratch=[pltpu.VMEM((width, depth), BF16), pltpu.SemaphoreType.DMA(())],
        specs=[VMEM, HBM] + [VMEM] * (len(pieces) + len(extra)),
        cost=cost,
        after=after,
    )(send, w_out, *pieces, *extra)
    return out


def regroup_body(peer, *refs):
    outs = refs[-(refs[0].shape[1] // peer) :]
    pieces = refs[: -len(outs)]
    for b, out in enumerate(outs):
        for a, piece in enumerate(pieces):
            out[:, a * peer : (a + 1) * peer] = piece[:, b * peer : (b + 1) * peer]


def regroup(pieces, peer, cost, after=()):
    heads, rows, width = pieces[0].shape
    outer = rows // peer
    if peer % 16:
        table = jnp.stack(pieces, 1).reshape(heads, len(pieces), outer, peer, width)
        return [table[:, :, b].reshape(heads, -1, width) for b in range(outer)]
    return call(
        functools.partial(regroup_body, peer),
        [((heads, len(pieces) * peer, width), BF16)] * outer,
        cost=cost,
        after=after,
    )(*pieces)


def swap(array, axis, by):
    if by == 0:
        return array
    return lax.ppermute(array, axis, [(i, i ^ by) for i in range(lax.axis_size(axis))])


def exchange(pieces, axis):
    out = {r: swap(pieces[r], axis, r) for r in reversed(range(len(pieces)))}
    return [out[r] for r in range(len(pieces))]


def all_exchange(rows, tok_rows):
    devices = lax.axis_size(AXES)
    if rows.shape[1] != tok_rows:
        return lax.all_to_all(rows, BLOCKS_ALONG, split_axis=0, concat_axis=0, tiled=True)
    split = rows.reshape(rows.shape[0], devices, tok_rows // devices, rows.shape[2])
    return lax.all_to_all(split, BLOCKS_ALONG, split_axis=1, concat_axis=1, tiled=True).reshape(rows.shape)


def per_device(tokens, norm_gain, w_qk, w_value, w_out, send_order, place):
    tok_rows = tokens.shape[0]
    n_sx, n_sy = lax.axis_size("sx"), lax.axis_size("sy")
    peer = tok_rows // (n_sx * n_sy)
    place = lax.ppermute(place, AXES, [(d, worker(d)) for d in range(n_sx * n_sy)])
    (leaving,) = project(tokens, norm_gain, send_order, w_qk, w_value, 0, HEADS, "", peer)
    arrived = all_exchange(leaving, tok_rows)
    (back,) = attention(place, [arrived], "", 0, HEADS, "", peer, 0)
    returned = all_exchange(back, tok_rows)
    return merge(send_order, w_out, None, [returned], 0, HEADS, "", peer, 0)


def solution(mesh):
    return jax.shard_map(
        per_device,
        mesh=mesh,
        in_specs=(
            P(AXES, None),
            P(),
            P(),
            P(),
            P(),
            P(None, AXES),
            P(None, AXES),
        ),
        out_specs=P(AXES, None),
        check_vma=False,
    )
```

time: 128 us -> 119 us (0.930)
  blocking collectives: 84 us -> 29.3 us
  waiting for transfers between devices: 15.2 us -> 45.1 us
  Pallas kernels: 0 us -> 29.6 us
  matrix products: 19.6 us -> 0 us
  starting transfers between devices: 0.06 us -> 13.2 us
  other arithmetic: 5.44 us -> 0 us
  local copies, waits for them, and re-layouts: 2.6 us -> 0.02 us
    all_to_all x2 -> x1, blocking collectives: 84 us -> 29.3 us  [all_exchange(): lax.all_to_all(rows, BLOCKS_ALONG, split_axis=0, concat_axis=0, tiled=True)]
    pallas_call x0 -> x5, Pallas kernels: none -> 29.6 us  [wrapped(): pl.pallas_call(skipping, out_shape=[jax.ShapeDtypeStruct(s, d) for s, d i...]
    all_to_all x0 -> x1, waiting for transfers between devices: none -> 23.4 us  [all_exchange(): lax.all_to_all(rows, BLOCKS_ALONG, split_axis=0, concat_axis=0, tiled=True)]
    dot_general x9 -> x0, matrix products: 19.6 us -> none  [the longest x1 3.15 us: per_device(): jnp.einsum('hip,hic->hpc', place_table, arrived, preferred_element_type=j...]
    all_to_all x0 -> x1, starting transfers between devices: none -> 7.1 us  [all_exchange(): lax.all_to_all(rows, BLOCKS_ALONG, split_axis=0, concat_axis=0, tiled=True)]
    ppermute x1 -> x2, waiting for transfers between devices: 15.2 us -> 21.7 us  [the longest x1 21.7 us: per_device(): lax.ppermute(place, AXES, [(d, worker(d)) for d in range(n_sx * n_sy)])]
    ppermute x1 -> x2, starting transfers between devices: 0.06 us -> 6.07 us  [the longest x1 3.54 us: per_device(): lax.ppermute(place, AXES, [(d, worker(d)) for d in range(n_sx * n_sy)])]
    reduce_sum x2 -> x0, other arithmetic: 2.82 us -> none  [the longest x1 1.65 us: per_device(): row_stat = jnp.mean(floats * floats, -1, keepdims=True) + 1e-06]
  transfers between devices with their start and end apart: 1 -> 3, of which waited for: 1 -> 2; matrix products, arithmetic and copies ran while one was open for 0% -> 0% of each run, Pallas kernels for 0% -> 7%
where the time goes in v1:
time: 119 us; the launch traced here: 117 us
  waiting for transfers between devices  45.1 us (38%)
  Pallas kernels  29.6 us (25%)
  blocking collectives  29.3 us (25%)
  starting transfers between devices  13.2 us (11%)
    pallas_call x5, Pallas kernels, wrapped(): pl.pallas_call(skipping, out_shape=[jax.ShapeDtypeStruct(s, d) for s, d i...  29.6 us
    all_to_all x1, blocking collectives, all_exchange(): lax.all_to_all(rows, BLOCKS_ALONG, split_axis=0, concat_axis=0, tiled=True)  29.3 us
    all_to_all x1, waiting for transfers between devices, all_exchange(): lax.all_to_all(rows, BLOCKS_ALONG, split_axis=0, concat_axis=0, tiled=True)  23.4 us
    ppermute x1, waiting for transfers between devices, per_device(): lax.ppermute(place, AXES, [(d, worker(d)) for d in range(n_sx * n_sy)])  21.7 us
    all_to_all x1, starting transfers between devices, all_exchange(): lax.all_to_all(rows, BLOCKS_ALONG, split_axis=0, concat_axis=0, tiled=True)  7.1 us
    ppermute x1, starting transfers between devices, per_device(): lax.ppermute(place, AXES, [(d, worker(d)) for d in range(n_sx * n_sy)])  3.54 us
    ppermute x1, starting transfers between devices, attention(): lax.ppermute(edge, AXES, [(worker(d), worker((d + 1) % peers)) for d in r...  2.52 us
  transfers between devices with their start and end apart: 3, of which 2 were waited for; matrix products, arithmetic and copies ran while one was open for 0% of the time, Pallas kernels for 7%

profile of v1, /device:TPU:1, one launch (start us, length us, event | category | flops | bytes accessed | tf_op | source)
XLA Modules:
  0.0 117.5 jit_solution(18369274611169626356)
XLA Ops:
  0.0 13.0 %shard_map.73 = bf16[32,128,256]{2,1,0:T(8,128)(2,1)} custom-call(bf16[512,1024]{1,0:T(8,128)(2,1)} %refs_0_.2, f32[1,1024]{1,0:T(1,128)} %bitcast.1, s32[8,512]{1,0:T(8,128)} %refs_0_.3, bf16[1024,1024]{1,0:T(8,128)(2,1)} %refs_3_.1, bf16[1024,1024]{1,0:T(8,128)(2,1)} %refs_4_.1), custom_call_target="tpu_custom_call" | custom-call | tf_op jit(solution)/shard_map/pallas_call | solution.py:86
  13.0 0.0 copy-start.2
  13.0 7.1 %all-to-all-start = ((bf16[32,128,256]{2,1,0:T(8,128)(2,1)}), bf16[32,128,256]{2,1,0:T(8,128)(2,1)S(1)}, u32[]{:S(2)}, u32[]{:S(2)}) async-start(bf16[32,128,256]{2,1,0:T(8,128)(2,1)} %shard_map.73), calls=%async_computation | async-start | bytes 4194304 | tf_op jit(solution)/shard_map/all_to_all | solution.py:345
  20.1 0.0 copy-done.2
  20.2 3.5 %collective-permute-start = (s32[8,512]{1,0:T(8,128)S(1)}, s32[8,512]{1,0:T(8,128)S(1)}, u32[]{:S(2)}, u32[]{:S(2)}) collective-permute-start(s32[8,512]{1,0:T(8,128)S(1)} %copy-done.2), channel_id=1, source_target_pairs={{0,0},{1,4},{2,8},{3,12},{4,16},{5,20},{6,24},{7,28},{8,1},{9,5},{... | collective-permute-start | bytes 49160 | tf_op jit(solution)/shard_map/ppermute | solution.py:354
  23.7 21.7 %collective-permute-done.refs_0_ = s32[8,512]{1,0:T(8,128)S(1)} collective-permute-done((s32[8,512]{1,0:T(8,128)S(1)}, s32[8,512]{1,0:T(8,128)S(1)}, u32[]{:S(2)}, u32[]{:S(2)}) %collective-permute-start) | collective-permute-done | bytes 16416 | tf_op jit(solution)/shard_map/ppermute | solution.py:354
  45.4 23.4 %all-to-all-done.refs_1_.refs_2_ = bf16[32,128,256]{2,1,0:T(8,128)(2,1)S(1)} async-done(((bf16[32,128,256]{2,1,0:T(8,128)(2,1)}), bf16[32,128,256]{2,1,0:T(8,128)(2,1)S(1)}, u32[]{:S(2)}, u32[]{:S(2)}) %all-to-all-start) | async-done | bytes 2097184 | tf_op jit(solution)/shard_map/all_to_all | solution.py:345
  68.8 0.7 shard_map.74.refs_1_
  69.5 2.5 %collective-permute-start.1 = (bf16[8,128,256]{2,1,0:T(8,128)(2,1)S(1)}, bf16[8,128,256]{2,1,0:T(8,128)(2,1)S(1)}, u32[]{:S(2)}, u32[]{:S(2)}) collective-permute-start(bf16[8,128,256]{2,1,0:T(8,128)(2,1)S(1)} %shard_map.74.refs_1_), channel_id=1, source_target_pairs={{0,4},{4,8},{8,12},{12,16},{16,20},{20,24},{24,28},{28,1},{1,5},{5... | collective-permute-start | bytes 1572872 | tf_op jit(solution)/shard_map/ppermute | solution.py:262
  72.0 8.6 %shard_map.75 = (bf16[8,128,256]{2,1,0:T(8,128)(2,1)S(1)}, bf16[8,384,128]{2,1,0:T(8,128)(2,1)S(1)}) custom-call(s32[8,512]{1,0:T(8,128)S(1)} %collective-permute-done.refs_0_, bf16[8,128,256]{2,1,0:T(8,128)(2,1)S(1)} %shard_map.74.refs_1_, bf16[32,128,256]{2,1,0:T(8,128)(2,1)S(1)} %all-to-all-done.refs_1_.refs_2_), custom_call_target="tpu_custom_call" | custom-call | tf_op jit(solution)/shard_map/pallas_call | solution.py:86
  80.6 0.0 collective-permute-done.1.refs_1_
  80.6 0.0 copy-start
  80.6 0.0 copy-start.1
  80.6 3.7 %shard_map.76 = bf16[32,128,128]{2,1,0:T(8,128)(2,1)S(1)} custom-call(s32[8,512]{1,0:T(8,128)S(1)} %collective-permute-done.refs_0_, bf16[8,128,256]{2,1,0:T(8,128)(2,1)S(1)} %collective-permute-done.1.refs_1_, bf16[8,128,256]{2,1,0:T(8,128)(2,1)S(1)} %get-tuple-element.7.refs_2_, bf16[8,384,128]{2,1,0:T(8,128)(2,1)S(1)} %get-tuple-element.8.refs_3_), custom_call_target="tpu_custom_call" | custom-call | tf_op jit(solution)/shard_map/pallas_call | solution.py:86
  84.4 29.3 %all_to_all.10.refs_2_ = bf16[32,128,128]{2,1,0:T(8,128)(2,1)S(1)} all-to-all(bf16[32,128,128]{2,1,0:T(8,128)(2,1)S(1)} %shard_map.76), channel_id=1, replica_groups=mesh['sx'=8,'sy'=4] {'sy','sx'}, dimensions={0} | all-to-all | bytes 2097152 | tf_op jit(solution)/shard_map/all_to_all | solution.py:345
  113.7 0.0 copy-done
  113.7 0.0 copy-done.1
  113.7 3.6 %shard_map.77 = bf16[512,1024]{1,0:T(8,128)(2,1)} custom-call(s32[8,512]{1,0:T(8,128)S(1)} %copy-done.1, bf16[1024,1024]{1,0:T(8,128)(2,1)S(1)} %copy-done, bf16[32,128,128]{2,1,0:T(8,128)(2,1)S(1)} %all_to_all.10.refs_2_), custom_call_target="tpu_custom_call" | custom-call | tf_op jit(solution)/shard_map/pallas_call | solution.py:86
Async XLA Ops:
  13.0 7.1 %copy-start.2 = (s32[8,512]{1,0:T(8,128)S(1)}, s32[8,512]{1,0:T(8,128)}, u32[]{:S(2)}) copy-start(s32[8,512]{1,0:T(8,128)} %param.13) | copy-start | bytes 49156
  13.0 55.7 %all-to-all-start = ((bf16[32,128,256]{2,1,0:T(8,128)(2,1)}), bf16[32,128,256]{2,1,0:T(8,128)(2,1)S(1)}, u32[]{:S(2)}, u32[]{:S(2)}) async-start(bf16[32,128,256]{2,1,0:T(8,128)(2,1)} %shard_map.73), calls=%async_computation | async-start | bytes 4194304 | tf_op jit(solution)/shard_map/all_to_all | solution.py:345
  20.2 25.2 %collective-permute-start = (s32[8,512]{1,0:T(8,128)S(1)}, s32[8,512]{1,0:T(8,128)S(1)}, u32[]{:S(2)}, u32[]{:S(2)}) collective-permute-start(s32[8,512]{1,0:T(8,128)S(1)} %copy-done.2), channel_id=1, source_target_pairs={{0,0},{1,4},{2,8},{3,12},{4,16},{5,20},{6,24},{7,28},{8,1},{9,5},{... | collective-permute-start | bytes 49160 | tf_op jit(solution)/shard_map/ppermute | solution.py:354
  69.5 11.1 %collective-permute-start.1 = (bf16[8,128,256]{2,1,0:T(8,128)(2,1)S(1)}, bf16[8,128,256]{2,1,0:T(8,128)(2,1)S(1)}, u32[]{:S(2)}, u32[]{:S(2)}) collective-permute-start(bf16[8,128,256]{2,1,0:T(8,128)(2,1)S(1)} %shard_map.74.refs_1_), channel_id=1, source_target_pairs={{0,4},{4,8},{8,12},{12,16},{16,20},{20,24},{24,28},{28,1},{1,5},{5... | collective-permute-start | bytes 1572872 | tf_op jit(solution)/shard_map/ppermute | solution.py:262
  80.6 33.1 %copy-start = (bf16[1024,1024]{1,0:T(8,128)(2,1)S(1)}, bf16[1024,1024]{1,0:T(8,128)(2,1)}, u32[]{:S(2)}) copy-start(bf16[1024,1024]{1,0:T(8,128)(2,1)} %refs_1_.1) | copy-start | bytes 6291460
  80.6 33.1 %copy-start.1 = (s32[8,512]{1,0:T(8,128)S(1)}, s32[8,512]{1,0:T(8,128)}, u32[]{:S(2)}) copy-start(s32[8,512]{1,0:T(8,128)} %refs_0_.3) | copy-start | bytes 49156

commit v2 on v0

v2 whole, which is shorter than its diff:
```python
import functools

import jax
import jax.numpy as jnp
from jax import lax
from jax.experimental import pallas as pl
from jax.experimental.pallas import tpu as pltpu
from jax.sharding import PartitionSpec as P

HEADS = 8
HEAD_DIM = 128
SPAN = 128
WIDTH = 2 * HEAD_DIM
AXES = ("sx", "sy")
MIB = 1024 * 1024
PARTS = 4
BF16 = jnp.bfloat16
F32 = jnp.float32
ANY = pl.BlockSpec(memory_space=pl.ANY)
HBM = pl.BlockSpec(memory_space=pltpu.HBM)
VMEM = pl.BlockSpec(memory_space=pltpu.VMEM)


def dot(a, b):
    return jnp.dot(a, b, preferred_element_type=F32)


def dot_first(a, b):
    return lax.dot_general(a, b, (((0,), (0,)), ((), ())), preferred_element_type=F32)


def dot_last(a, b):
    return lax.dot_general(a, b, (((1,), (1,)), ((), ())), preferred_element_type=F32)


def one_hot(row, first, size):
    sublanes = lax.broadcasted_iota(jnp.int32, (size, row.shape[1]), 0) + first
    return jnp.where(sublanes == row, 1.0, 0.0).astype(BF16)


def call(body, outs, scratch=(), specs=None, out_specs=None, limit=40, cost=0, after=()):
    count = [0]

    def skipping(*refs):
        return body(*refs[: count[0]], *refs[count[0] + len(after) :])

    def wrapped(*args):
        count[0] = len(args)
        return pl.pallas_call(
            skipping,
            out_shape=[jax.ShapeDtypeStruct(s, d) for s, d in outs],
            in_specs=([VMEM] * len(args) if specs is None else specs) + [ANY] * len(after),
            out_specs=[VMEM] * len(outs) if out_specs is None else out_specs,
            scratch_shapes=list(scratch),
            compiler_params=pltpu.CompilerParams(vmem_limit_bytes=limit * MIB),
            cost_estimate=pl.CostEstimate(flops=cost, bytes_accessed=0, transcendentals=0),
        )(*args, *after)

    return wrapped


def block_rows(arrived, b, peer):
    if peer % 16:
        return arrived[b]
    own = slice(b * peer, (b + 1) * peer)
    return jnp.concatenate([arrived[s, own] for s in range(arrived.shape[0])], 0)


def place_of(place, block):
    me = lax.axis_index("sx") * lax.axis_size("sy") + lax.axis_index("sy")
    return place[pl.ds((me & (HEADS - 1)) ^ block, 1), :]


def project_body(tokens, gain, send, w_qk, w_value, out, *scratch):
    held, normed, by_head, moved, wq, wv, token_sems, sems, out_sems = scratch
    rows, depth = held.shape
    block = rows // PARTS
    loads = []
    for i in range(PARTS):
        part = pl.ds(i * block, block)
        loads.append(pltpu.make_async_copy(tokens.at[part], held.at[part], token_sems.at[i]))
        loads[-1].start()
    copies = []
    for j, (source, target) in enumerate(((w_qk, wq), (w_value, wv))):
        for i in range(2):
            cols = pl.ds(i * depth // 2, depth // 2)
            copies.append(
                pltpu.make_async_copy(source.at[:, cols], target.at[:, cols], sems.at[2 * j + i])
            )
    for i in (0, 2, 1, 3):
        copies[i].start()
    for i in range(PARTS):
        loads[i].wait()
        part = slice(i * block, (i + 1) * block)
        floats = held[part].astype(F32)
        stat = jnp.sum(floats * floats, -1, keepdims=True) * (1.0 / depth) + 1e-06
        normed[part] = (floats * lax.rsqrt(stat) * gain[...]).astype(BF16)
    for p in range(HEADS // 2):
        if p % (HEADS // 4) == 0:
            i = p // (HEADS // 4)
            copies[i].wait()
            copies[2 + i].wait()
        cols = slice(p * WIDTH, (p + 1) * WIDTH)
        for j, weights in enumerate((wq, wv)):
            both = dot(normed[...], weights[:, cols]).astype(BF16)
            side = slice(j * HEAD_DIM, (j + 1) * HEAD_DIM)
            by_head[2 * p, :, side] = both[:, :HEAD_DIM]
            by_head[2 * p + 1, :, side] = both[:, HEAD_DIM:]
    stores = []
    runs, size = moved.shape[1], moved.shape[2]
    for h in range(HEADS):
        table = one_hot(send[h : h + 1, :], 0, rows)
        rows_of_head = dot_first(table, by_head[h]).astype(BF16)
        for g in range(runs):
            moved[h, g] = rows_of_head[g * size : (g + 1) * size]
        stores.append(pltpu.make_async_copy(moved.at[h], out.at[:, h], out_sems.at[h]))
        stores[-1].start()
    for store in stores:
        store.wait()


def edge_body(peer, place, arrived, out):
    rows = place.shape[1]
    table = one_hot(place_of(place, HEADS - 1), rows - SPAN, SPAN)
    out[...] = dot(table, block_rows(arrived, HEADS - 1, peer)).astype(BF16)


def unit_keys(shared):
    keys = shared.astype(F32)
    stat = jnp.sum(keys * keys, -1, keepdims=True) + 1e-06
    return (keys * lax.rsqrt(stat)).astype(BF16)


def one_span(query, unit, values):
    root = HEAD_DIM**0.5
    scores = dot_last(unit, query)
    keys = lax.broadcasted_iota(jnp.int32, scores.shape, 0)
    queries = lax.broadcasted_iota(jnp.int32, scores.shape, 1)
    scores = jnp.where(keys == queries + SPAN, -100000.0 * root, scores)
    shifted = scores - jnp.max(scores, 0, keepdims=True)
    powers = jnp.exp2(shifted * (1.4426950408889634 / root))
    weights = (powers * (1.0 / jnp.sum(powers, 0, keepdims=True))).astype(BF16)
    return dot_first(weights, values).astype(BF16)


def store_block(out, moved, b, peer):
    if peer % 16:
        out[b] = moved
        return
    for s in range(out.shape[0]):
        out[s, b * peer : (b + 1) * peer] = moved[s * peer : (s + 1) * peer]


def inner_body(peer, place, arrived, head_span, first_block, leaving, ordered, unit, attended):
    rows = place.shape[1]
    for b in range(HEADS):
        table = one_hot(place_of(place, b), 0, rows)
        ordered[b * rows : (b + 1) * rows] = dot(table, block_rows(arrived, b, peer)).astype(BF16)
    for b in range(HEADS):
        part = slice(b * rows, (b + 1) * rows)
        unit[part] = unit_keys(ordered[part, :HEAD_DIM])
    head_span[...] = ordered[:SPAN]
    attended[:SPAN] = jnp.zeros((SPAN, HEAD_DIM), BF16)
    for c in range(1, HEADS * rows // SPAN):
        own = slice(c * SPAN, (c + 1) * SPAN)
        window = slice((c - 1) * SPAN, (c + 1) * SPAN)
        attended[own] = one_span(ordered[own, :HEAD_DIM], unit[window], ordered[window, HEAD_DIM:])
    for b in range(HEADS):
        table = one_hot(place_of(place, b), 0, rows)
        moved = dot_first(table, attended[b * rows : (b + 1) * rows]).astype(BF16)
        if b:
            store_block(leaving, moved, b, peer)
        else:
            first_block[...] = moved


def outer_body(peer, place, before, head_span, first_block, leaving, out, window, unit, attended):
    window[:SPAN] = before[...]
    window[SPAN:] = head_span[...]
    unit[...] = unit_keys(window[:, :HEAD_DIM])
    attended[...] = one_span(head_span[:, :HEAD_DIM], unit[...], window[:, HEAD_DIM:])
    moved = dot_first(one_hot(place_of(place, 0), 0, SPAN), attended[...]).astype(BF16)
    store_block(out, first_block[...] + moved, 0, peer)
    if peer % 16:
        out[1:] = leaving[1:]
    else:
        out[:, peer:] = leaving[:, peer:]


def merge_body(send, arrived, w_out, out, merged, result, sems):
    rows = send.shape[1]
    runs = arrived.shape[0] // HEADS
    for h in range(HEADS):
        table = one_hot(send[h : h + 1, :], 0, rows)
        cols = slice(h * HEAD_DIM, (h + 1) * HEAD_DIM)
        rows_of_head = jnp.concatenate([arrived[g * HEADS + h] for g in range(runs)], 0)
        merged[:, cols] = dot(table, rows_of_head).astype(BF16)
    block = rows // PARTS
    copies = []
    for i in range(PARTS):
        part = slice(i * block, (i + 1) * block)
        result[part] = dot(merged[part], w_out[...]).astype(BF16)
        copies.append(
            pltpu.make_async_copy(
                result.at[pl.ds(i * block, block)], out.at[pl.ds(i * block, block)], sems.at[i]
            )
        )
        copies[-1].start()
    for copy in copies:
        copy.wait()


def by_block(rows, peer):
    if peer % 16 == 0:
        return rows
    devices, size, width = rows.shape
    split = rows.reshape(devices, size // peer, peer, width).transpose(1, 0, 2, 3)
    return split.reshape(size // peer, devices * peer, width)


def by_device(rows, peer):
    if peer % 16 == 0:
        return rows
    blocks, size, width = rows.shape
    split = rows.reshape(blocks, size // peer, peer, width).transpose(1, 0, 2, 3)
    return split.reshape(size // peer, blocks * peer, width)


def exchange(rows):
    return lax.all_to_all(rows, AXES, split_axis=0, concat_axis=0, tiled=True)


def per_device(tokens, norm_gain, w_qk, w_value, w_out, send_order, place):
    rows, depth = tokens.shape
    devices = lax.axis_size(AXES)
    peer = rows // devices
    runs = devices // HEADS
    me = lax.axis_index(AXES) % HEADS

    def turned(table, bit):
        split = table.reshape(HEADS // (2 * bit), 2, bit, rows)
        return jnp.where((me & bit) > 0, jnp.flip(split, 1), split).reshape(HEADS, rows)

    def traded(table, by):
        return lax.ppermute(table, AXES, [(i, i ^ by) for i in range(devices)])

    half = HEADS // 2
    place = turned(place, half)
    near, far = place[:half], traded(place[half:], half)
    place = jnp.concatenate([near, far], 0)
    bit = 1
    while bit < half:
        place = turned(place, bit)
        bit *= 2
    place = place.reshape(2, half, rows)
    parts = [traded(place[:, r], r) if r else place[:, r] for r in range(half)]
    place = jnp.stack(parts, 1).reshape(HEADS, rows)

    (leaving,) = call(
        project_body,
        [((runs, HEADS, rows // runs, WIDTH), BF16)],
        scratch=[
            pltpu.VMEM((rows, depth), BF16),
            pltpu.VMEM((rows, depth), BF16),
            pltpu.VMEM((HEADS, rows, WIDTH), BF16),
            pltpu.VMEM((HEADS, runs, rows // runs, WIDTH), BF16),
            pltpu.VMEM(w_qk.shape, BF16),
            pltpu.VMEM(w_value.shape, BF16),
            pltpu.SemaphoreType.DMA((PARTS,)),
            pltpu.SemaphoreType.DMA((4,)),
            pltpu.SemaphoreType.DMA((HEADS,)),
        ],
        specs=[HBM, VMEM, VMEM, HBM, HBM],
        out_specs=[HBM],
        limit=60,
        cost=2 * rows * HEADS * WIDTH * (depth + rows),
    )(tokens, norm_gain.reshape(1, depth), send_order, w_qk, w_value)
    arrived = exchange(leaving.reshape(devices, rows // runs, WIDTH))
    arrived = by_block(arrived, peer)
    (edge,) = call(functools.partial(edge_body, peer), [((SPAN, WIDTH), BF16)])(place, arrived)
    onward = [(i, (i + HEADS) % devices) for i in range(devices)]
    before = lax.ppermute(edge, AXES, onward)
    gone = (HEADS, rows, HEAD_DIM) if peer % 16 else (devices, HEADS * peer, HEAD_DIM)
    head_span, first_block, partly = call(
        functools.partial(inner_body, peer),
        [((SPAN, WIDTH), BF16), ((rows, HEAD_DIM), BF16), (gone, BF16)],
        scratch=[
            pltpu.VMEM((HEADS * rows, WIDTH), BF16),
            pltpu.VMEM((HEADS * rows, HEAD_DIM), BF16),
            pltpu.VMEM((HEADS * rows, HEAD_DIM), BF16),
        ],
        after=[edge],
    )(place, arrived)
    (back,) = call(
        functools.partial(outer_body, peer),
        [(gone, BF16)],
        scratch=[
            pltpu.VMEM((2 * SPAN, WIDTH), BF16),
            pltpu.VMEM((2 * SPAN, HEAD_DIM), BF16),
            pltpu.VMEM((SPAN, HEAD_DIM), BF16),
        ],
    )(place, before, head_span, first_block, partly)
    returned = exchange(by_device(back, peer))
    (out,) = call(
        merge_body,
        [((rows, w_out.shape[1]), BF16)],
        scratch=[
            pltpu.VMEM((rows, HEADS * HEAD_DIM), BF16),
            pltpu.VMEM((rows, w_out.shape[1]), BF16),
            pltpu.SemaphoreType.DMA((PARTS,)),
        ],
        out_specs=[HBM],
        limit=20,
    )(send_order, returned, w_out)
    return out


def solution(mesh):
    return jax.shard_map(
        per_device,
        mesh=mesh,
        in_specs=(
            P(AXES, None),
            P(),
            P(),
            P(),
            P(),
            P(None, AXES),
            P(None, AXES),
        ),
        out_specs=P(AXES, None),
        check_vma=False,
    )
```

time: 128 us -> 103 us (0.80)
  blocking collectives: 84 us -> 29.4 us
  waiting for transfers between devices: 15.2 us -> 44.4 us
  matrix products: 19.6 us -> 0 us
  Pallas kernels: 0 us -> 15.9 us
  starting transfers between devices: 0.06 us -> 12.6 us
  other arithmetic: 5.44 us -> 0.06 us
  local copies, waits for them, and re-layouts: 2.6 us -> 0.29 us
    all_to_all x2 -> x1, blocking collectives: 84 us -> 29.4 us  [exchange(): return lax.all_to_all(rows, AXES, split_axis=0, concat_axis=0, tiled=True)]
    ppermute x1 -> x5, waiting for transfers between devices: 15.2 us -> 44.4 us  [the longest x4 44.4 us: traded(): return lax.ppermute(table, AXES, [(i, i ^ by) for i in range(devices)])]
    dot_general x9 -> x0, matrix products: 19.6 us -> none  [the longest x1 3.15 us: per_device(): jnp.einsum('hip,hic->hpc', place_table, arrived, preferred_element_type=j...]
    pallas_call x0 -> x5, Pallas kernels: none -> 15.9 us  [wrapped(): pl.pallas_call(skipping, out_shape=[jax.ShapeDtypeStruct(s, d) for s, d i...]
    all_to_all x0 -> x1, starting transfers between devices: none -> 7.11 us  [exchange(): return lax.all_to_all(rows, AXES, split_axis=0, concat_axis=0, tiled=True)]
    ppermute x1 -> x5, starting transfers between devices: 0.06 us -> 5.46 us  [the longest x4 4.01 us: traded(): return lax.ppermute(table, AXES, [(i, i ^ by) for i in range(devices)])]
    reduce_sum x2 -> x0, other arithmetic: 2.82 us -> none  [the longest x1 1.65 us: per_device(): row_stat = jnp.mean(floats * floats, -1, keepdims=True) + 1e-06]
    sub x1 -> x0, other arithmetic: 2 us -> none  [attend_spans(): weights = jax.nn.softmax(scores, axis=-1).astype(jnp.bfloat16)]
  transfers between devices with their start and end apart: 1 -> 6, of which waited for: 1 -> 3; matrix products, arithmetic and copies ran while one was open for 0% -> 0% of each run, Pallas kernels for 0% -> 4%
where the time goes in v2:
time: 103 us
  waiting for transfers between devices  44.4 us (43%)
  blocking collectives  29.4 us (29%)
  Pallas kernels  15.9 us (15%)
  starting transfers between devices  12.6 us (12%)
    ppermute x4, waiting for transfers between devices, traded(): return lax.ppermute(table, AXES, [(i, i ^ by) for i in range(devices)])  44.4 us
    all_to_all x1, blocking collectives, exchange(): return lax.all_to_all(rows, AXES, split_axis=0, concat_axis=0, tiled=True)  29.4 us
    pallas_call x5, Pallas kernels, wrapped(): pl.pallas_call(skipping, out_shape=[jax.ShapeDtypeStruct(s, d) for s, d i...  15.9 us
    all_to_all x1, starting transfers between devices, exchange(): return lax.all_to_all(rows, AXES, split_axis=0, concat_axis=0, tiled=True)  7.11 us
    ppermute x4, starting transfers between devices, traded(): return lax.ppermute(table, AXES, [(i, i ^ by) for i in range(devices)])  4.01 us
  transfers between devices with their start and end apart: 6, of which 3 were waited for; matrix products, arithmetic and copies ran while one was open for 0% of the time, Pallas kernels for 4%

profile of v2, /device:TPU:1, one launch (start us, length us, event | category | flops | bytes accessed | tf_op | source)
XLA Modules:
  0.0 102.8 jit_solution(2970112650403658728)
XLA Ops:
  0.0 7.7 %shard_map.73 = bf16[4,8,128,256]{3,2,1,0:T(8,128)(2,1)} custom-call(bf16[512,1024]{1,0:T(8,128)(2,1)} %refs_0_.2, f32[1,1024]{1,0:T(1,128)} %bitcast.26, s32[8,512]{1,0:T(8,128)} %refs_0_.3, bf16[1024,1024]{1,0:T(8,128)(2,1)} %refs_3_.1, bf16[1024,1024]{1,0:T(8,128)(2,1)} %refs_4_.1), custom_call_target="tpu_custom_call" | custom-call | flops 3221225472 | tf_op jit(solution)/shard_map/pallas_call | solution.py:49
  7.7 0.0 copy-start.2
  7.7 7.1 %all-to-all-start = ((bf16[32,128,256]{2,1,0:T(8,128)(2,1)}), bf16[32,128,256]{2,1,0:T(8,128)(2,1)S(1)}, u32[]{:S(2)}, u32[]{:S(2)}) async-start(bf16[32,128,256]{2,1,0:T(8,128)(2,1)} %bitcast.19), calls=%async_computation | async-start | bytes 4194304 | tf_op jit(solution)/shard_map/all_to_all | solution.py:230
  14.8 0.0 copy-done.2
  14.9 0.3 collective-permute-start
  15.2 0.9 collective-permute-done
  16.1 0.2 rev.13
  16.4 3.3 %collective-permute-start.3 = (s32[2,512]{1,0:T(2,128)S(1)}, s32[2,512]{1,0:T(2,128)S(1)}, u32[]{:S(2)}, u32[]{:S(2)}) collective-permute-start(s32[2,512]{1,0:T(2,128)S(1)} %bitcast.25), channel_id=1, source_target_pairs={{0,3},{1,2},{2,1},{3,0},{4,7},{5,6},{6,5},{7,4},{8,11},{9,10},{10,... | collective-permute-start | bytes 12296 | tf_op jit(solution)/shard_map/ppermute | solution.py:245
  19.8 0.0 collective-permute-start.1
  19.8 0.4 collective-permute-start.2
  20.1 33.4 %collective-permute-done.3 = s32[2,512]{1,0:T(2,128)S(1)} collective-permute-done((s32[2,512]{1,0:T(2,128)S(1)}, s32[2,512]{1,0:T(2,128)S(1)}, u32[]{:S(2)}, u32[]{:S(2)}) %collective-permute-start.3) | collective-permute-done | bytes 4128 | tf_op jit(solution)/shard_map/ppermute | solution.py:245
  53.5 0.0 collective-permute-done.1
  53.5 10.2 %collective-permute-done.2 = s32[2,512]{1,0:T(2,128)S(1)} collective-permute-done((s32[2,512]{1,0:T(2,128)S(1)}, s32[2,512]{1,0:T(2,128)S(1)}, u32[]{:S(2)}, u32[]{:S(2)}) %collective-permute-start.2) | collective-permute-done | bytes 4128 | tf_op jit(solution)/shard_map/ppermute | solution.py:245
  63.7 0.0 all-to-all-done.refs_1_
  63.7 0.2 shard_map.74.refs_2_
  63.9 1.5 %collective-permute-start.4 = (bf16[128,256]{1,0:T(8,128)(2,1)S(1)}, bf16[128,256]{1,0:T(8,128)(2,1)S(1)}, u32[]{:S(2)}, u32[]{:S(2)}) collective-permute-start(bf16[128,256]{1,0:T(8,128)(2,1)S(1)} %shard_map.74.refs_2_), channel_id=1, source_target_pairs={{0,8},{1,9},{2,10},{3,11},{4,12},{5,13},{6,14},{7,15},{8,16},{9,17... | collective-permute-start | bytes 196616 | tf_op jit(solution)/shard_map/ppermute | solution.py:282
  65.4 4.2 %shard_map.75 = (bf16[128,256]{1,0:T(8,128)(2,1)S(1)}, bf16[512,128]{1,0:T(8,128)(2,1)S(1)}, bf16[32,128,128]{2,1,0:T(8,128)(2,1)S(1)}) custom-call(s32[8,512]{1,0:T(8,128)S(1)} %reshape.20.refs_0_, bf16[32,128,256]{2,1,0:T(8,128)(2,1)S(1)} %all-to-all-done.refs_1_, bf16[128,256]{1,0:T(8,128)(2,1)S(1)} %shard_map.74.refs_2_), custom_call_target="tpu_custom_call" | custom-call | tf_op jit(solution)/shard_map/pallas_call | solution.py:49
  69.6 0.0 collective-permute-done.4.refs_1_
  69.6 0.0 copy-start
  69.6 0.0 copy-start.1
  69.6 0.7 shard_map.76
  70.3 29.4 %all_to_all.10.refs_1_ = bf16[32,128,128]{2,1,0:T(8,128)(2,1)S(1)} all-to-all(bf16[32,128,128]{2,1,0:T(8,128)(2,1)S(1)} %shard_map.76), channel_id=1, replica_groups=mesh['sx'=8,'sy'=4] {'sx','sy'}, dimensions={0} | all-to-all | bytes 2097152 | tf_op jit(solution)/shard_map/all_to_all | solution.py:230
  99.7 0.0 copy-done.1
  99.7 3.1 %shard_map.77 = bf16[512,1024]{1,0:T(8,128)(2,1)} custom-call(s32[8,512]{1,0:T(8,128)S(1)} %copy-done.1, bf16[32,128,128]{2,1,0:T(8,128)(2,1)S(1)} %all_to_all.10.refs_1_, bf16[1024,1024]{1,0:T(8,128)(2,1)S(1)} %copy-done), custom_call_target="tpu_custom_call" | custom-call | tf_op jit(solution)/shard_map/pallas_call | solution.py:49
  (18 shorter events, 0.2 us)
Async XLA Ops:
  7.7 7.1 %copy-start.2 = (s32[8,512]{1,0:T(8,128)S(1)}, s32[8,512]{1,0:T(8,128)}, u32[]{:S(2)}) copy-start(s32[8,512]{1,0:T(8,128)} %param.13) | copy-start | bytes 49156
  7.7 56.0 %all-to-all-start = ((bf16[32,128,256]{2,1,0:T(8,128)(2,1)}), bf16[32,128,256]{2,1,0:T(8,128)(2,1)S(1)}, u32[]{:S(2)}, u32[]{:S(2)}) async-start(bf16[32,128,256]{2,1,0:T(8,128)(2,1)} %bitcast.19), calls=%async_computation | async-start | bytes 4194304 | tf_op jit(solution)/shard_map/all_to_all | solution.py:230
  14.9 1.2 %collective-permute-start = (s32[4,512]{1,0:T(4,128)S(1)}, s32[4,512]{1,0:T(4,128)S(1)}, u32[]{:S(2)}, u32[]{:S(2)}) collective-permute-start(s32[4,512]{1,0:T(4,128)S(1)} %get-tuple-element.16), channel_id=1, source_target_pairs={{0,4},{1,5},{2,6},{3,7},{4,0},{5,1},{6,2},{7,3},{8,12},{9,13},{10,... | collective-permute-start | bytes 24584 | tf_op jit(solution)/shard_map/ppermute | solution.py:245
  16.4 37.0 %collective-permute-start.3 = (s32[2,512]{1,0:T(2,128)S(1)}, s32[2,512]{1,0:T(2,128)S(1)}, u32[]{:S(2)}, u32[]{:S(2)}) collective-permute-start(s32[2,512]{1,0:T(2,128)S(1)} %bitcast.25), channel_id=1, source_target_pairs={{0,3},{1,2},{2,1},{3,0},{4,7},{5,6},{6,5},{7,4},{8,11},{9,10},{10,... | collective-permute-start | bytes 12296 | tf_op jit(solution)/shard_map/ppermute | solution.py:245
  19.8 33.7 %collective-permute-start.1 = (s32[2,512]{1,0:T(2,128)S(1)}, s32[2,512]{1,0:T(2,128)S(1)}, u32[]{:S(2)}, u32[]{:S(2)}) collective-permute-start(s32[2,512]{1,0:T(2,128)S(1)} %bitcast.24), channel_id=1, source_target_pairs={{0,1},{1,0},{2,3},{3,2},{4,5},{5,4},{6,7},{7,6},{8,9},{9,8},{10,11... | collective-permute-start | bytes 12296 | tf_op jit(solution)/shard_map/ppermute | solution.py:245
  19.8 43.9 %collective-permute-start.2 = (s32[2,512]{1,0:T(2,128)S(1)}, s32[2,512]{1,0:T(2,128)S(1)}, u32[]{:S(2)}, u32[]{:S(2)}) collective-permute-start(s32[2,512]{1,0:T(2,128)S(1)} %bitcast.23), channel_id=1, source_target_pairs={{0,2},{1,3},{2,0},{3,1},{4,6},{5,7},{6,4},{7,5},{8,10},{9,11},{10,... | collective-permute-start | bytes 12296 | tf_op jit(solution)/shard_map/ppermute | solution.py:245
  63.9 5.7 %collective-permute-start.4 = (bf16[128,256]{1,0:T(8,128)(2,1)S(1)}, bf16[128,256]{1,0:T(8,128)(2,1)S(1)}, u32[]{:S(2)}, u32[]{:S(2)}) collective-permute-start(bf16[128,256]{1,0:T(8,128)(2,1)S(1)} %shard_map.74.refs_2_), channel_id=1, source_target_pairs={{0,8},{1,9},{2,10},{3,11},{4,12},{5,13},{6,14},{7,15},{8,16},{9,17... | collective-permute-start | bytes 196616 | tf_op jit(solution)/shard_map/ppermute | solution.py:282
  69.6 30.1 %copy-start = (bf16[1024,1024]{1,0:T(8,128)(2,1)S(1)}, bf16[1024,1024]{1,0:T(8,128)(2,1)}, u32[]{:S(2)}) copy-start(bf16[1024,1024]{1,0:T(8,128)(2,1)} %refs_2_.3) | copy-start | bytes 6291460
  69.6 30.1 %copy-start.1 = (s32[8,512]{1,0:T(8,128)S(1)}, s32[8,512]{1,0:T(8,128)}, u32[]{:S(2)}) copy-start(s32[8,512]{1,0:T(8,128)} %refs_0_.3) | copy-start | bytes 49156

commit v3 on v2

--- a/solution.py
+++ b/solution.py
@@ -89,23 +89,40 @@
             )
     for i in (0, 2, 1, 3):
         copies[i].start()
-    for i in range(PARTS):
+    def norm(i):
         loads[i].wait()
+        norm_rest(i)
+
+    def norm_rest(i):
         part = slice(i * block, (i + 1) * block)
         floats = held[part].astype(F32)
         stat = jnp.sum(floats * floats, -1, keepdims=True) * (1.0 / depth) + 1e-06
         normed[part] = (floats * lax.rsqrt(stat) * gain[...]).astype(BF16)
-    for p in range(HEADS // 2):
-        if p % (HEADS // 4) == 0:
-            i = p // (HEADS // 4)
-            copies[i].wait()
-            copies[2 + i].wait()
-        cols = slice(p * WIDTH, (p + 1) * WIDTH)
-        for j, weights in enumerate((wq, wv)):
-            both = dot(normed[...], weights[:, cols]).astype(BF16)
-            side = slice(j * HEAD_DIM, (j + 1) * HEAD_DIM)
-            by_head[2 * p, :, side] = both[:, :HEAD_DIM]
-            by_head[2 * p + 1, :, side] = both[:, HEAD_DIM:]
+
+    def multiply(part, pairs):
+        for p in pairs:
+            cols = slice(p * WIDTH, (p + 1) * WIDTH)
+            for j, weights in enumerate((wq, wv)):
+                both = dot(normed[part], weights[:, cols]).astype(BF16)
+                side = slice(j * HEAD_DIM, (j + 1) * HEAD_DIM)
+                by_head[2 * p, part, side] = both[:, :HEAD_DIM]
+                by_head[2 * p + 1, part, side] = both[:, HEAD_DIM:]
+
+    early, late = range(HEADS // 4), range(HEADS // 4, HEADS // 2)
+    top, bottom = slice(0, rows // 2), slice(rows // 2, rows)
+    for i in range(PARTS // 2):
+        norm(i)
+    copies[0].wait()
+    copies[2].wait()
+    for i in range(PARTS // 2, PARTS):
+        loads[i].wait()
+    multiply(top, early)
+    for i in range(PARTS // 2, PARTS):
+        norm_rest(i)
+    multiply(bottom, early)
+    copies[1].wait()
+    copies[3].wait()
+    multiply(slice(0, rows), late)
     stores = []
     runs, size = moved.shape[1], moved.shape[2]
     for h in range(HEADS):

time: 103 us -> 103 us (level)
  no operation moved by 1% of the time
where the time goes in v3:
time: 103 us
  waiting for transfers between devices  44.4 us (43%)
  blocking collectives  29.4 us (29%)
  Pallas kernels  15.7 us (15%)
  starting transfers between devices  12.6 us (12%)
    ppermute x4, waiting for transfers between devices, traded(): return lax.ppermute(table, AXES, [(i, i ^ by) for i in range(devices)])  44.4 us
    all_to_all x1, blocking collectives, exchange(): return lax.all_to_all(rows, AXES, split_axis=0, concat_axis=0, tiled=True)  29.4 us
    pallas_call x5, Pallas kernels, wrapped(): pl.pallas_call(skipping, out_shape=[jax.ShapeDtypeStruct(s, d) for s, d i...  15.7 us
    all_to_all x1, starting transfers between devices, exchange(): return lax.all_to_all(rows, AXES, split_axis=0, concat_axis=0, tiled=True)  7.1 us
    ppermute x4, starting transfers between devices, traded(): return lax.ppermute(table, AXES, [(i, i ^ by) for i in range(devices)])  4.01 us
  transfers between devices with their start and end apart: 6, of which 3 were waited for; matrix products, arithmetic and copies ran while one was open for 0% of the time, Pallas kernels for 4%

profile of v3, /device:TPU:1, one launch (start us, length us, event | category | flops | bytes accessed | tf_op | source)
XLA Modules:
  0.0 102.7 jit_solution(11137866437454398862)
XLA Ops:
  0.0 7.5 %shard_map.73 = bf16[4,8,128,256]{3,2,1,0:T(8,128)(2,1)} custom-call(bf16[512,1024]{1,0:T(8,128)(2,1)} %refs_0_.2, f32[1,1024]{1,0:T(1,128)} %bitcast.26, s32[8,512]{1,0:T(8,128)} %refs_0_.3, bf16[1024,1024]{1,0:T(8,128)(2,1)} %refs_3_.1, bf16[1024,1024]{1,0:T(8,128)(2,1)} %refs_4_.1), custom_call_target="tpu_custom_call" | custom-call | flops 3221225472 | tf_op jit(solution)/shard_map/pallas_call | solution.py:49
  7.5 0.0 copy-start.2
  7.6 7.1 %all-to-all-start = ((bf16[32,128,256]{2,1,0:T(8,128)(2,1)}), bf16[32,128,256]{2,1,0:T(8,128)(2,1)S(1)}, u32[]{:S(2)}, u32[]{:S(2)}) async-start(bf16[32,128,256]{2,1,0:T(8,128)(2,1)} %bitcast.19), calls=%async_computation | async-start | bytes 4194304 | tf_op jit(solution)/shard_map/all_to_all | solution.py:247
  14.7 0.0 copy-done.2
  14.7 0.3 collective-permute-start
  15.1 0.9 collective-permute-done
  16.0 0.2 rev.13
  16.3 3.3 %collective-permute-start.3 = (s32[2,512]{1,0:T(2,128)S(1)}, s32[2,512]{1,0:T(2,128)S(1)}, u32[]{:S(2)}, u32[]{:S(2)}) collective-permute-start(s32[2,512]{1,0:T(2,128)S(1)} %bitcast.25), channel_id=1, source_target_pairs={{0,3},{1,2},{2,1},{3,0},{4,7},{5,6},{6,5},{7,4},{8,11},{9,10},{10,... | collective-permute-start | bytes 12296 | tf_op jit(solution)/shard_map/ppermute | solution.py:262
  19.6 0.0 collective-permute-start.1
  19.6 0.4 collective-permute-start.2
  20.0 33.4 %collective-permute-done.3 = s32[2,512]{1,0:T(2,128)S(1)} collective-permute-done((s32[2,512]{1,0:T(2,128)S(1)}, s32[2,512]{1,0:T(2,128)S(1)}, u32[]{:S(2)}, u32[]{:S(2)}) %collective-permute-start.3) | collective-permute-done | bytes 4128 | tf_op jit(solution)/shard_map/ppermute | solution.py:262
  53.3 0.0 collective-permute-done.1
  53.4 10.2 %collective-permute-done.2 = s32[2,512]{1,0:T(2,128)S(1)} collective-permute-done((s32[2,512]{1,0:T(2,128)S(1)}, s32[2,512]{1,0:T(2,128)S(1)}, u32[]{:S(2)}, u32[]{:S(2)}) %collective-permute-start.2) | collective-permute-done | bytes 4128 | tf_op jit(solution)/shard_map/ppermute | solution.py:262
  63.6 0.0 all-to-all-done.refs_1_
  63.6 0.2 shard_map.74.refs_2_
  63.8 1.5 %collective-permute-start.4 = (bf16[128,256]{1,0:T(8,128)(2,1)S(1)}, bf16[128,256]{1,0:T(8,128)(2,1)S(1)}, u32[]{:S(2)}, u32[]{:S(2)}) collective-permute-start(bf16[128,256]{1,0:T(8,128)(2,1)S(1)} %shard_map.74.refs_2_), channel_id=1, source_target_pairs={{0,8},{1,9},{2,10},{3,11},{4,12},{5,13},{6,14},{7,15},{8,16},{9,17... | collective-permute-start | bytes 196616 | tf_op jit(solution)/shard_map/ppermute | solution.py:299
  65.2 4.2 %shard_map.75 = (bf16[128,256]{1,0:T(8,128)(2,1)S(1)}, bf16[512,128]{1,0:T(8,128)(2,1)S(1)}, bf16[32,128,128]{2,1,0:T(8,128)(2,1)S(1)}) custom-call(s32[8,512]{1,0:T(8,128)S(1)} %reshape.20.refs_0_, bf16[32,128,256]{2,1,0:T(8,128)(2,1)S(1)} %all-to-all-done.refs_1_, bf16[128,256]{1,0:T(8,128)(2,1)S(1)} %shard_map.74.refs_2_), custom_call_target="tpu_custom_call" | custom-call | tf_op jit(solution)/shard_map/pallas_call | solution.py:49
  69.4 0.0 collective-permute-done.4.refs_1_
  69.4 0.0 copy-start
  69.4 0.0 copy-start.1
  69.4 0.7 shard_map.76
  70.2 29.4 %all_to_all.10.refs_1_ = bf16[32,128,128]{2,1,0:T(8,128)(2,1)S(1)} all-to-all(bf16[32,128,128]{2,1,0:T(8,128)(2,1)S(1)} %shard_map.76), channel_id=1, replica_groups=mesh['sx'=8,'sy'=4] {'sx','sy'}, dimensions={0} | all-to-all | bytes 2097152 | tf_op jit(solution)/shard_map/all_to_all | solution.py:247
  99.5 0.0 copy-done
  99.6 3.1 %shard_map.77 = bf16[512,1024]{1,0:T(8,128)(2,1)} custom-call(s32[8,512]{1,0:T(8,128)S(1)} %copy-done.1, bf16[32,128,128]{2,1,0:T(8,128)(2,1)S(1)} %all_to_all.10.refs_1_, bf16[1024,1024]{1,0:T(8,128)(2,1)S(1)} %copy-done), custom_call_target="tpu_custom_call" | custom-call | tf_op jit(solution)/shard_map/pallas_call | solution.py:49
  (18 shorter events, 0.2 us)
Async XLA Ops:
  7.5 7.1 %copy-start.2 = (s32[8,512]{1,0:T(8,128)S(1)}, s32[8,512]{1,0:T(8,128)}, u32[]{:S(2)}) copy-start(s32[8,512]{1,0:T(8,128)} %param.13) | copy-start | bytes 49156
  7.6 56.0 %all-to-all-start = ((bf16[32,128,256]{2,1,0:T(8,128)(2,1)}), bf16[32,128,256]{2,1,0:T(8,128)(2,1)S(1)}, u32[]{:S(2)}, u32[]{:S(2)}) async-start(bf16[32,128,256]{2,1,0:T(8,128)(2,1)} %bitcast.19), calls=%async_computation | async-start | bytes 4194304 | tf_op jit(solution)/shard_map/all_to_all | solution.py:247
  14.7 1.2 %collective-permute-start = (s32[4,512]{1,0:T(4,128)S(1)}, s32[4,512]{1,0:T(4,128)S(1)}, u32[]{:S(2)}, u32[]{:S(2)}) collective-permute-start(s32[4,512]{1,0:T(4,128)S(1)} %get-tuple-element.16), channel_id=1, source_target_pairs={{0,4},{1,5},{2,6},{3,7},{4,0},{5,1},{6,2},{7,3},{8,12},{9,13},{10,... | collective-permute-start | bytes 24584 | tf_op jit(solution)/shard_map/ppermute | solution.py:262
  16.3 37.0 %collective-permute-start.3 = (s32[2,512]{1,0:T(2,128)S(1)}, s32[2,512]{1,0:T(2,128)S(1)}, u32[]{:S(2)}, u32[]{:S(2)}) collective-permute-start(s32[2,512]{1,0:T(2,128)S(1)} %bitcast.25), channel_id=1, source_target_pairs={{0,3},{1,2},{2,1},{3,0},{4,7},{5,6},{6,5},{7,4},{8,11},{9,10},{10,... | collective-permute-start | bytes 12296 | tf_op jit(solution)/shard_map/ppermute | solution.py:262
  19.6 33.7 %collective-permute-start.1 = (s32[2,512]{1,0:T(2,128)S(1)}, s32[2,512]{1,0:T(2,128)S(1)}, u32[]{:S(2)}, u32[]{:S(2)}) collective-permute-start(s32[2,512]{1,0:T(2,128)S(1)} %bitcast.24), channel_id=1, source_target_pairs={{0,1},{1,0},{2,3},{3,2},{4,5},{5,4},{6,7},{7,6},{8,9},{9,8},{10,11... | collective-permute-start | bytes 12296 | tf_op jit(solution)/shard_map/ppermute | solution.py:262
  19.6 43.9 %collective-permute-start.2 = (s32[2,512]{1,0:T(2,128)S(1)}, s32[2,512]{1,0:T(2,128)S(1)}, u32[]{:S(2)}, u32[]{:S(2)}) collective-permute-start(s32[2,512]{1,0:T(2,128)S(1)} %bitcast.23), channel_id=1, source_target_pairs={{0,2},{1,3},{2,0},{3,1},{4,6},{5,7},{6,4},{7,5},{8,10},{9,11},{10,... | collective-permute-start | bytes 12296 | tf_op jit(solution)/shard_map/ppermute | solution.py:262
  63.8 5.7 %collective-permute-start.4 = (bf16[128,256]{1,0:T(8,128)(2,1)S(1)}, bf16[128,256]{1,0:T(8,128)(2,1)S(1)}, u32[]{:S(2)}, u32[]{:S(2)}) collective-permute-start(bf16[128,256]{1,0:T(8,128)(2,1)S(1)} %shard_map.74.refs_2_), channel_id=1, source_target_pairs={{0,8},{1,9},{2,10},{3,11},{4,12},{5,13},{6,14},{7,15},{8,16},{9,17... | collective-permute-start | bytes 196616 | tf_op jit(solution)/shard_map/ppermute | solution.py:299
  69.4 30.1 %copy-start = (bf16[1024,1024]{1,0:T(8,128)(2,1)S(1)}, bf16[1024,1024]{1,0:T(8,128)(2,1)}, u32[]{:S(2)}) copy-start(bf16[1024,1024]{1,0:T(8,128)(2,1)} %refs_2_.3) | copy-start | bytes 6291460
  69.4 30.1 %copy-start.1 = (s32[8,512]{1,0:T(8,128)S(1)}, s32[8,512]{1,0:T(8,128)}, u32[]{:S(2)}) copy-start(s32[8,512]{1,0:T(8,128)} %refs_0_.3) | copy-start | bytes 49156

commit v4 on v3

--- a/solution.py
+++ b/solution.py
@@ -14,6 +14,7 @@
 AXES = ("sx", "sy")
 MIB = 1024 * 1024
 PARTS = 4
+STORES = 2
 BF16 = jnp.bfloat16
 F32 = jnp.float32
 ANY = pl.BlockSpec(memory_space=pl.ANY)
@@ -212,9 +213,9 @@
         cols = slice(h * HEAD_DIM, (h + 1) * HEAD_DIM)
         rows_of_head = jnp.concatenate([arrived[g * HEADS + h] for g in range(runs)], 0)
         merged[:, cols] = dot(table, rows_of_head).astype(BF16)
-    block = rows // PARTS
+    block = rows // STORES
     copies = []
-    for i in range(PARTS):
+    for i in range(STORES):
         part = slice(i * block, (i + 1) * block)
         result[part] = dot(merged[part], w_out[...]).astype(BF16)
         copies.append(
@@ -324,7 +325,7 @@
         scratch=[
             pltpu.VMEM((rows, HEADS * HEAD_DIM), BF16),
             pltpu.VMEM((rows, w_out.shape[1]), BF16),
-            pltpu.SemaphoreType.DMA((PARTS,)),
+            pltpu.SemaphoreType.DMA((STORES,)),
         ],
         out_specs=[HBM],
         limit=20,

time: 103 us -> 103 us (level)
  no operation moved by 1% of the time
where the time goes in v4:
time: 103 us
  waiting for transfers between devices  44.4 us (43%)
  blocking collectives  29.4 us (29%)
  Pallas kernels  15.8 us (15%)
  starting transfers between devices  12.6 us (12%)
    ppermute x4, waiting for transfers between devices, traded(): return lax.ppermute(table, AXES, [(i, i ^ by) for i in range(devices)])  44.4 us
    all_to_all x1, blocking collectives, exchange(): return lax.all_to_all(rows, AXES, split_axis=0, concat_axis=0, tiled=True)  29.4 us
    pallas_call x5, Pallas kernels, wrapped(): pl.pallas_call(skipping, out_shape=[jax.ShapeDtypeStruct(s, d) for s, d i...  15.8 us
    all_to_all x1, starting transfers between devices, exchange(): return lax.all_to_all(rows, AXES, split_axis=0, concat_axis=0, tiled=True)  7.1 us
    ppermute x4, starting transfers between devices, traded(): return lax.ppermute(table, AXES, [(i, i ^ by) for i in range(devices)])  4.01 us
  transfers between devices with their start and end apart: 6, of which 3 were waited for; matrix products, arithmetic and copies ran while one was open for 0% of the time, Pallas kernels for 4%

profile of v4, /device:TPU:1, one launch (start us, length us, event | category | flops | bytes accessed | tf_op | source)
XLA Modules:
  0.0 102.7 jit_solution(3272571838011821172)
XLA Ops:
  0.0 7.5 %shard_map.73 = bf16[4,8,128,256]{3,2,1,0:T(8,128)(2,1)} custom-call(bf16[512,1024]{1,0:T(8,128)(2,1)} %refs_0_.2, f32[1,1024]{1,0:T(1,128)} %bitcast.26, s32[8,512]{1,0:T(8,128)} %refs_0_.3, bf16[1024,1024]{1,0:T(8,128)(2,1)} %refs_3_.1, bf16[1024,1024]{1,0:T(8,128)(2,1)} %refs_4_.1), custom_call_target="tpu_custom_call" | custom-call | flops 3221225472 | tf_op jit(solution)/shard_map/pallas_call | solution.py:50
  7.5 0.0 copy-start.2
  7.6 7.1 %all-to-all-start = ((bf16[32,128,256]{2,1,0:T(8,128)(2,1)}), bf16[32,128,256]{2,1,0:T(8,128)(2,1)S(1)}, u32[]{:S(2)}, u32[]{:S(2)}) async-start(bf16[32,128,256]{2,1,0:T(8,128)(2,1)} %bitcast.19), calls=%async_computation | async-start | bytes 4194304 | tf_op jit(solution)/shard_map/all_to_all | solution.py:248
  14.7 0.0 copy-done.2
  14.7 0.3 collective-permute-start
  15.1 0.9 collective-permute-done
  16.0 0.2 rev.13
  16.3 3.3 %collective-permute-start.3 = (s32[2,512]{1,0:T(2,128)S(1)}, s32[2,512]{1,0:T(2,128)S(1)}, u32[]{:S(2)}, u32[]{:S(2)}) collective-permute-start(s32[2,512]{1,0:T(2,128)S(1)} %bitcast.25), channel_id=1, source_target_pairs={{0,3},{1,2},{2,1},{3,0},{4,7},{5,6},{6,5},{7,4},{8,11},{9,10},{10,... | collective-permute-start | bytes 12296 | tf_op jit(solution)/shard_map/ppermute | solution.py:263
  19.6 0.0 collective-permute-start.1
  19.6 0.4 collective-permute-start.2
  20.0 33.4 %collective-permute-done.3 = s32[2,512]{1,0:T(2,128)S(1)} collective-permute-done((s32[2,512]{1,0:T(2,128)S(1)}, s32[2,512]{1,0:T(2,128)S(1)}, u32[]{:S(2)}, u32[]{:S(2)}) %collective-permute-start.3) | collective-permute-done | bytes 4128 | tf_op jit(solution)/shard_map/ppermute | solution.py:263
  53.3 0.0 collective-permute-done.1
  53.4 10.2 %collective-permute-done.2 = s32[2,512]{1,0:T(2,128)S(1)} collective-permute-done((s32[2,512]{1,0:T(2,128)S(1)}, s32[2,512]{1,0:T(2,128)S(1)}, u32[]{:S(2)}, u32[]{:S(2)}) %collective-permute-start.2) | collective-permute-done | bytes 4128 | tf_op jit(solution)/shard_map/ppermute | solution.py:263
  63.6 0.0 all-to-all-done.refs_1_
  63.6 0.2 shard_map.74.refs_2_
  63.8 1.5 %collective-permute-start.4 = (bf16[128,256]{1,0:T(8,128)(2,1)S(1)}, bf16[128,256]{1,0:T(8,128)(2,1)S(1)}, u32[]{:S(2)}, u32[]{:S(2)}) collective-permute-start(bf16[128,256]{1,0:T(8,128)(2,1)S(1)} %shard_map.74.refs_2_), channel_id=1, source_target_pairs={{0,8},{1,9},{2,10},{3,11},{4,12},{5,13},{6,14},{7,15},{8,16},{9,17... | collective-permute-start | bytes 196616 | tf_op jit(solution)/shard_map/ppermute | solution.py:300
  65.2 4.2 %shard_map.75 = (bf16[128,256]{1,0:T(8,128)(2,1)S(1)}, bf16[512,128]{1,0:T(8,128)(2,1)S(1)}, bf16[32,128,128]{2,1,0:T(8,128)(2,1)S(1)}) custom-call(s32[8,512]{1,0:T(8,128)S(1)} %reshape.20.refs_0_, bf16[32,128,256]{2,1,0:T(8,128)(2,1)S(1)} %all-to-all-done.refs_1_, bf16[128,256]{1,0:T(8,128)(2,1)S(1)} %shard_map.74.refs_2_), custom_call_target="tpu_custom_call" | custom-call | tf_op jit(solution)/shard_map/pallas_call | solution.py:50
  69.4 0.0 collective-permute-done.4.refs_1_
  69.4 0.0 copy-start
  69.4 0.0 copy-start.1
  69.4 0.7 shard_map.76
  70.2 29.4 %all_to_all.10.refs_1_ = bf16[32,128,128]{2,1,0:T(8,128)(2,1)S(1)} all-to-all(bf16[32,128,128]{2,1,0:T(8,128)(2,1)S(1)} %shard_map.76), channel_id=1, replica_groups=mesh['sx'=8,'sy'=4] {'sx','sy'}, dimensions={0} | all-to-all | bytes 2097152 | tf_op jit(solution)/shard_map/all_to_all | solution.py:248
  99.5 0.0 copy-done
  99.6 3.2 %shard_map.77 = bf16[512,1024]{1,0:T(8,128)(2,1)} custom-call(s32[8,512]{1,0:T(8,128)S(1)} %copy-done.1, bf16[32,128,128]{2,1,0:T(8,128)(2,1)S(1)} %all_to_all.10.refs_1_, bf16[1024,1024]{1,0:T(8,128)(2,1)S(1)} %copy-done), custom_call_target="tpu_custom_call" | custom-call | tf_op jit(solution)/shard_map/pallas_call | solution.py:50
  (18 shorter events, 0.2 us)
Async XLA Ops:
  7.5 7.1 %copy-start.2 = (s32[8,512]{1,0:T(8,128)S(1)}, s32[8,512]{1,0:T(8,128)}, u32[]{:S(2)}) copy-start(s32[8,512]{1,0:T(8,128)} %param.13) | copy-start | bytes 49156
  7.6 56.0 %all-to-all-start = ((bf16[32,128,256]{2,1,0:T(8,128)(2,1)}), bf16[32,128,256]{2,1,0:T(8,128)(2,1)S(1)}, u32[]{:S(2)}, u32[]{:S(2)}) async-start(bf16[32,128,256]{2,1,0:T(8,128)(2,1)} %bitcast.19), calls=%async_computation | async-start | bytes 4194304 | tf_op jit(solution)/shard_map/all_to_all | solution.py:248
  14.7 1.2 %collective-permute-start = (s32[4,512]{1,0:T(4,128)S(1)}, s32[4,512]{1,0:T(4,128)S(1)}, u32[]{:S(2)}, u32[]{:S(2)}) collective-permute-start(s32[4,512]{1,0:T(4,128)S(1)} %get-tuple-element.16), channel_id=1, source_target_pairs={{0,4},{1,5},{2,6},{3,7},{4,0},{5,1},{6,2},{7,3},{8,12},{9,13},{10,... | collective-permute-start | bytes 24584 | tf_op jit(solution)/shard_map/ppermute | solution.py:263
  16.3 37.0 %collective-permute-start.3 = (s32[2,512]{1,0:T(2,128)S(1)}, s32[2,512]{1,0:T(2,128)S(1)}, u32[]{:S(2)}, u32[]{:S(2)}) collective-permute-start(s32[2,512]{1,0:T(2,128)S(1)} %bitcast.25), channel_id=1, source_target_pairs={{0,3},{1,2},{2,1},{3,0},{4,7},{5,6},{6,5},{7,4},{8,11},{9,10},{10,... | collective-permute-start | bytes 12296 | tf_op jit(solution)/shard_map/ppermute | solution.py:263
  19.6 33.7 %collective-permute-start.1 = (s32[2,512]{1,0:T(2,128)S(1)}, s32[2,512]{1,0:T(2,128)S(1)}, u32[]{:S(2)}, u32[]{:S(2)}) collective-permute-start(s32[2,512]{1,0:T(2,128)S(1)} %bitcast.24), channel_id=1, source_target_pairs={{0,1},{1,0},{2,3},{3,2},{4,5},{5,4},{6,7},{7,6},{8,9},{9,8},{10,11... | collective-permute-start | bytes 12296 | tf_op jit(solution)/shard_map/ppermute | solution.py:263
  19.6 43.9 %collective-permute-start.2 = (s32[2,512]{1,0:T(2,128)S(1)}, s32[2,512]{1,0:T(2,128)S(1)}, u32[]{:S(2)}, u32[]{:S(2)}) collective-permute-start(s32[2,512]{1,0:T(2,128)S(1)} %bitcast.23), channel_id=1, source_target_pairs={{0,2},{1,3},{2,0},{3,1},{4,6},{5,7},{6,4},{7,5},{8,10},{9,11},{10,... | collective-permute-start | bytes 12296 | tf_op jit(solution)/shard_map/ppermute | solution.py:263
  63.8 5.7 %collective-permute-start.4 = (bf16[128,256]{1,0:T(8,128)(2,1)S(1)}, bf16[128,256]{1,0:T(8,128)(2,1)S(1)}, u32[]{:S(2)}, u32[]{:S(2)}) collective-permute-start(bf16[128,256]{1,0:T(8,128)(2,1)S(1)} %shard_map.74.refs_2_), channel_id=1, source_target_pairs={{0,8},{1,9},{2,10},{3,11},{4,12},{5,13},{6,14},{7,15},{8,16},{9,17... | collective-permute-start | bytes 196616 | tf_op jit(solution)/shard_map/ppermute | solution.py:300
  69.4 30.1 %copy-start = (bf16[1024,1024]{1,0:T(8,128)(2,1)S(1)}, bf16[1024,1024]{1,0:T(8,128)(2,1)}, u32[]{:S(2)}) copy-start(bf16[1024,1024]{1,0:T(8,128)(2,1)} %refs_2_.3) | copy-start | bytes 6291460
  69.4 30.1 %copy-start.1 = (s32[8,512]{1,0:T(8,128)S(1)}, s32[8,512]{1,0:T(8,128)}, u32[]{:S(2)}) copy-start(s32[8,512]{1,0:T(8,128)} %refs_0_.3) | copy-start | bytes 49156
